TPU v7x, 128 devices: a whole 4x4x4 slice. The times are simulated.
128 devices in a mesh: row: 8 (over z, y_lo), col: 16 (over x, y_hi, core).
Axes of the slice: x: 4, y: 4 (y_hi: 2, y_lo: 2; y = y_hi * 2 + y_lo), z: 4, core: 2. Of those that a mesh axis runs over, the one named last changes fastest.
Arguments:
- inverse_anc: bfloat16 [16384, 16384], P('row', 'col'), may hold values from -6 to 6
- factor_panel: bfloat16 [16384, 4096], P('row', 'col'), may hold values from -0.046875 to 0.046875
- pattern: int32 [16, 64], replicated, may hold values 0 or 1
- diag_inverse: float32 [16, 256, 256], P('col'), may hold values from -6 to 6
Outputs:
- upper: bfloat16 [4096, 16384], P('col', 'row')
- diag_block: float32 [16, 256, 256], P('col')
All inputs are finite; a program needn't handle non-finite values.
Results may differ from a plain program's by a relative error of at most 0.0095.
Values may be sent and summed in bfloat16 or wider, within the bound.
A program may use at most 192 MiB of HBM per device.

v0:
```python
import jax
import jax.numpy as jnp
from jax import lax
from jax.sharding import PartitionSpec as P

SUPER = 256


def local(inverse_anc, factor_panel, pattern, diag_inverse):
    rows_here = factor_panel.shape[0]
    cols_here = factor_panel.shape[1]
    leaves_here = cols_here // SUPER
    blocks_here = rows_here // SUPER
    row_index = lax.axis_index("row")
    col_index = lax.axis_index("col")
    local_pattern = lax.dynamic_slice(
        pattern, (col_index * leaves_here, row_index * blocks_here), (leaves_here, blocks_here)
    )
    mask_upper = jnp.repeat(jnp.repeat(local_pattern, SUPER, axis=0), SUPER, axis=1)
    masked = factor_panel * mask_upper.T.astype(jnp.bfloat16)
    panel = lax.all_gather(masked, "row", axis=0, tiled=True)
    spread = lax.all_to_all(panel, "col", split_axis=0, concat_axis=1, tiled=True)
    summed = lax.psum_scatter(
        lax.dot_general(
            spread, inverse_anc, (((0,), (1,)), ((), ())), preferred_element_type=jnp.float32
        ),
        "col",
        scatter_dimension=0,
        tiled=True,
    )
    upper = (-summed * mask_upper.astype(jnp.float32)).astype(jnp.bfloat16)
    left = masked.astype(jnp.float32).reshape(rows_here, leaves_here, SUPER)
    right = upper.astype(jnp.float32).reshape(leaves_here, SUPER, rows_here)
    partial_diag = jnp.einsum("akw,kva->kwv", left, right, precision=lax.Precision.HIGHEST)
    correction = lax.psum(partial_diag.astype(jnp.bfloat16), "row").astype(jnp.float32)
    return (upper, diag_inverse - correction)


def solution(mesh):
    return jax.shard_map(
        local,
        mesh=mesh,
        in_specs=(P("row", "col"), P("row", "col"), P(), P("col", None, None)),
        out_specs=(P("col", "row"), P("col", None, None)),
        check_vma=False,
    )
```

profile of v0, /device:TPU:0, one launch (start us, length us, event | category | flops | bytes accessed | tf_op | source)
XLA Modules:
  0.0 651.9 jit_solution(11785005747557362593)
XLA Ops:
  7.2 0.0 all-gather.2.cloned.1.call-start
  7.2 0.8 convert_bitcast_fusion
  8.0 0.1 broadcast_bitcast_fusion.1
  8.1 2.5 broadcast_multiply_fusion
  10.6 0.0 all-gather.2.cloned.1.call-update
  10.6 0.0 reduce-scatter.2.cloned.1.call-start
  10.7 170.9 %all-gather.2.cloned.1.call-done = bf16[16384,256]{1,0:T(8,128)(2,1)} async-done(((bf16[2048,256]{1,0:T(8,128)(2,1)}), bf16[16384,256]{1,0:T(8,128)(2,1)}) %all-gather.2.cloned.1.call-update) | async-done | bytes 8388624 | tf_op jit(solution)/shard_map/all_gather | solution.py:21
  181.6 103.2 %all_to_all.19 = bf16[16,1024,256]{2,1,0:T(8,128)(2,1)} all-to-all(bf16[16,1024,256]{2,1,0:T(8,128)(2,1)} %bitcast.20), channel_id=1, replica_groups=mesh['row'=8,'col'=16] {'col'}, dimensions={0} | all-to-all | bytes 16777216 | tf_op jit(solution)/shard_map/all_to_all | solution.py:22
  284.9 12.3 %copy.6 = bf16[1024,16,256]{0,2,1:T(8,128)(2,1)} copy(bf16[1024,16,256]{2,0,1:T(8,128)(2,1)} %bitcast.19) | data formatting | bytes 16777216 | tf_op jit(solution)/shard_map/all_to_all | solution.py:22
  297.1 25.2 %fusion.1 = f32[4096,2048]{1,0:T(8,128)} fusion(bf16[1024,4096]{0,1:T(8,128)(2,1)} %bitcast.21, bf16[2048,1024]{1,0:T(8,128)(2,1)} %param.4), kind=kOutput, calls=%fused_computation.9 | convolution fusion | flops 17179869184 | bytes 46137344 | tf_op jit(solution)/shard_map/dot_general | solution.py:24
  322.3 0.0 copy-start
  322.3 0.0 reduce-scatter.2.cloned.1.call-update
  322.3 0.0 copy-start.2
  322.4 0.0 all-reduce.2.cloned.1.call-start
  322.4 0.1 broadcast_bitcast_fusion
  322.5 244.8 %reduce-scatter.2.cloned.1.call-done = f32[256,2048]{1,0:T(8,128)} async-done(((f32[4096,2048]{1,0:T(8,128)}), f32[256,2048]{1,0:T(8,128)}) %reduce-scatter.2.cloned.1.call-update) | async-done | bytes 2097168 | tf_op jit(solution)/shard_map/reduce_scatter | solution.py:23
  567.2 1.8 multiply_convert_fusion
  569.1 0.0 copy-done
  569.1 0.0 copy-start.1
  569.1 1.1 fusion
  570.2 0.0 all-reduce.2.cloned.1.call-update
  570.2 73.5 %all-reduce.2.cloned.1.call-done = bf16[1,256,256]{2,1,0:T(8,128)(2,1)} async-done(((bf16[1,256,256]{2,1,0:T(8,128)(2,1)}), bf16[1,256,256]{2,1,0:T(8,128)(2,1)}) %all-reduce.2.cloned.1.call-update) | async-done | bytes 131088 | tf_op jit(solution)/shard_map/psum | solution.py:35
  643.7 0.0 copy-done.2
  643.7 1.6 convert_subtract_fusion
  645.3 0.0 copy-done.1
  (2 shorter events, 0.0 us)
Async XLA Ops:
  7.2 174.4 %all-gather.2.cloned.1.call-start = ((), (), s32[]{:S(2)}) async-start(), calls=%async_computation.2 | async-start | bytes 9437184 | tf_op jit(solution)/shard_map/all_gather | solution.py:21
  10.6 556.6 %reduce-scatter.2.cloned.1.call-start = ((), (), s32[]{:S(2)}) async-start(), calls=%async_computation.3 | async-start | bytes 35651584 | tf_op jit(solution)/shard_map/reduce_scatter | solution.py:23
  322.3 246.7 %copy-start = (bf16[2048,256]{1,0:T(8,128)(2,1)S(1)}, bf16[2048,256]{1,0:T(8,128)(2,1)}, u32[]{:S(2)}) copy-start(bf16[2048,256]{1,0:T(8,128)(2,1)} %broadcast_multiply_fusion) | copy-start | bytes 3145732
  322.3 321.4 %copy-start.2 = (f32[1,256,256]{2,1,0:T(8,128)S(1)}, f32[1,256,256]{2,1,0:T(8,128)}, u32[]{:S(2)}) copy-start(f32[1,256,256]{2,1,0:T(8,128)} %param.7) | copy-start | bytes 786436
  322.4 321.4 %all-reduce.2.cloned.1.call-start = ((), (), s32[]{:S(2)}) async-start(), calls=%async_computation.4 | async-start | bytes 262144 | tf_op jit(solution)/shard_map/psum | solution.py:35
  569.1 76.3 %copy-start.1 = (bf16[256,2048]{1,0:T(8,128)(2,1)}, bf16[256,2048]{1,0:T(8,128)(2,1)S(1)}, u32[]{:S(2)}) copy-start(bf16[256,2048]{1,0:T(8,128)(2,1)S(1)} %multiply_convert_fusion) | copy-start | bytes 3145732
Sparse Core Ops, SparseCore 0:
  10.7 170.8 all-gather.1
  322.5 244.7 reduce-scatter.1
  570.4 73.2 all-reduce.1
where the time goes:
time: 652 us
  waiting for transfers between devices  489 us (75%)
  blocking collectives  103 us (16%)
  matrix products  26.3 us (4%)
  between operations  13.8 us (2%)
  local copies, waits for them, and re-layouts  12.4 us (2%)
  other arithmetic  6.74 us (1%)
    reduce_scatter x1, waiting for transfers between devices, local(): lax.psum_scatter(lax.dot_general(spread, inverse_anc, (((0,), (1,)), ((),...  245 us
    all_gather x1, waiting for transfers between devices, local(): panel = lax.all_gather(masked, 'row', axis=0, tiled=True)  171 us
    all_to_all x1, blocking collectives, local(): lax.all_to_all(panel, 'col', split_axis=0, concat_axis=1, tiled=True)  103 us
    psum x1, waiting for transfers between devices, local(): lax.psum(partial_diag.astype(jnp.bfloat16), 'row').astype(jnp.float32)  73.5 us
    dot_general x1, matrix products, local(): lax.dot_general(spread, inverse_anc, (((0,), (1,)), ((), ())), preferred_...  25.2 us
  transfers between devices with their start and end apart: 3, of which 3 were waited for; matrix products, arithmetic and copies ran while one was open for 0% of the time, Pallas kernels for 0%

commit v1 on v0

v1 whole, which is shorter than its diff:
```python
import functools

import jax
import jax.numpy as jnp
from jax import lax
from jax.experimental import pallas as pl
from jax.experimental.pallas import tpu as pltpu
from jax.sharding import PartitionSpec as P

SUPER = 256
ROWS = 2048
HALF = 1024
NSUB = 16
SUB = 128
CH = 32
HC = 16
TILE = 256
BF = jnp.bfloat16
F32 = jnp.float32
MESH = pl.DeviceIdType.MESH

ORDER = [
    (0, 0, 0), (0, 0, 1),
    (1, 0, 0), (2, 0, 0), (0, 1, 0),
    (1, 0, 1), (2, 0, 1), (0, 1, 1),
    (3, 0, 0), (1, 1, 0), (2, 1, 0), (3, 1, 0),
    (3, 0, 1), (1, 1, 1), (2, 1, 1), (3, 1, 1),
]
BATCHES = [(0, 1), (1, 1), (2, 3), (5, 3), (8, 1), (9, 3), (12, 1), (13, 3)]
ZOFF = {0: 0, 1: 3, 2: 1, 3: 2}


def kernel(
    a_ref, f_ref, pat_ref, dinv_ref,
    u_ref, diag_ref,
    afull, mt, mask, tz, m, p, pown, ra, rb, da, db, ea, eb, s2, ysend, yrecv, dsend, drecv, dfin,
    a_sem, tz_s, tz_r, tx_s, tx_r, m_s, m_r, rs_s, rs_r, y_s, y_r, d_s, d_r,
):
    row = lax.axis_index("row")
    col = lax.axis_index("col")
    z, yl = row // 2, row % 2
    x, yh, h = col // 4, (col // 2) % 2, col % 2

    def dev(z=z, yl=yl, x=x, yh=yh, h=h):
        return (z * 2 + yl, (x * 2 + yh) * 2 + h)

    def remote(src, dst, ssem, rsem, to):
        return pltpu.make_async_remote_copy(
            src_ref=src, dst_ref=dst, send_sem=ssem, recv_sem=rsem, device_id=to, device_id_type=MESH
        )

    def arrive(ref, sem):
        pltpu.make_async_copy(ref, ref, sem).wait()

    sends = []

    def send(src, dst, ssem, rsem, to):
        copy = remote(src, dst, ssem, rsem, to)
        copy.start()
        sends.append(copy)

    zp, zm = (z + 1) % 4, (z + 3) % 4
    xp, xm = (x + 1) % 4, (x + 3) % 4

    barrier = pltpu.get_barrier_semaphore()
    partners = [dev(h=1 - h), dev(yh=1 - yh)]
    for dz in range(4):
        for fl in range(2):
            if dz or fl:
                partners.append(dev(z=(z + dz) % 4, yl=(yl + fl) % 2))
    for dx in range(4):
        for fl in range(2):
            if dx or fl:
                partners.append(dev(x=(x + dx) % 4, yl=(yl + fl) % 2, yh=(yh + fl) % 2))
    for to in partners:
        pl.semaphore_signal(barrier, inc=1, device_id=to, device_id_type=MESH)

    a_local = pltpu.make_async_copy(a_ref, afull.at[h], a_sem.at[0])
    a_local.start()

    for b in range(8):
        keep = pat_ref[col, row * 8 + b].astype(F32)
        mask[:, b * 256:(b + 1) * 256] = jnp.full((8, 256), keep, F32)
        block = f_ref[b * 256:(b + 1) * 256, :].astype(F32)
        mt[:, b * 256:(b + 1) * 256] = (block.T * keep).astype(BF)

    pl.semaphore_wait(barrier, len(partners))

    def piece(zz, g):
        return mt.at[pl.ds(pl.multiple_of(zz * 64 + g * CH, CH), CH)]

    for dz in (1, 3, 2):
        zz = (z + dz) % 4
        k = (4 - dz) % 4
        send(piece(zz, 0), tz.at[0, k], tz_s.at[0, k], tz_r.at[0, k], dev(z=zz))
    for dz in (0, 1, 3, 2):
        zz = (z + dz) % 4
        k = (4 - dz) % 4
        send(piece(zz, 1), tz.at[1, k], tz_s.at[1, k], tz_r.at[1, k], dev(z=zz, yl=1 - yl))
    send(a_ref, afull.at[h], a_sem.at[1], a_sem.at[2], dev(h=1 - h))

    tx_waits = []
    for g in range(2):
        nyh, nyl = (yl, yh) if g == 0 else (1 - yl, 1 - yh)
        same_y = yl == yh if g == 0 else yl != yh
        for k in (0, 1, 3, 2):
            if g == 0 and k == 0:
                src = piece(z, 0)
            else:
                src = tz.at[g, k]
                arrive(src, tz_r.at[g, k])
            xd = (z + k) % 4
            slot = (x + 4 - xd) % 4
            dst = m.at[pl.ds(pl.multiple_of(g * SUB + slot * CH, CH), CH)]
            far = remote(src, dst, tx_s.at[g, k], tx_r.at[g], dev(x=xd, yh=nyh, yl=nyl))
            near = pltpu.make_async_copy(src, dst, tx_r.at[g])
            here = jnp.logical_and(same_y, xd == x)

            @pl.when(here)
            def _():
                near.start()

            @pl.when(jnp.logical_not(here))
            def _():
                far.start()

            tx_waits.append((here, far))

    def msub(s, lo=0, n=SUB):
        return m.at[s * SUB + lo:s * SUB + lo + n]

    def multiply(s0, n):
        rows = slice(s0 * SUB, (s0 + n) * SUB)

        def tile(it, carry):
            at = pl.ds(pl.multiple_of(it * TILE, TILE), TILE)
            dims = (((1,), (1,)), ((), ()))
            acc = lax.dot_general(m[rows, :HALF], afull[0, at, :], dims, preferred_element_type=F32)
            acc += lax.dot_general(m[rows, HALF:], afull[1, at, :], dims, preferred_element_type=F32)
            for i in range(n):
                pown[s0 + i, :, at] = acc[i * SUB:i * SUB + CH]
                p[s0 + i, :, at] = acc[i * SUB + CH:(i + 1) * SUB].astype(BF)
            return carry

        lax.fori_loop(0, ROWS // TILE, tile, 0)

    def reduce_1(s):
        send(p.at[s, 32:48], ra.at[s], rs_s.at[s, 0], rs_r.at[s, 0], dev(x=xp))
        send(p.at[s, 48:64], rb.at[s], rs_s.at[s, 1], rs_r.at[s, 1], dev(x=xm))
        send(p.at[s, 16:32], db.at[s], rs_s.at[s, 2], rs_r.at[s, 2], dev(x=xp))
        send(p.at[s, 64:80], da.at[s], rs_s.at[s, 3], rs_r.at[s, 3], dev(x=xm))

    def reduce_2(s):
        arrive(ra.at[s], rs_r.at[s, 0])
        p[s, 0:16] = (p[s, 0:16].astype(F32) + ra[s].astype(F32)).astype(BF)
        send(p.at[s, 0:16], ea.at[s], rs_s.at[s, 4], rs_r.at[s, 4], dev(x=xp))
        arrive(rb.at[s], rs_r.at[s, 1])
        p[s, 80:96] = (p[s, 80:96].astype(F32) + rb[s].astype(F32)).astype(BF)
        send(p.at[s, 80:96], eb.at[s], rs_s.at[s, 5], rs_r.at[s, 5], dev(x=xm))

    def reduce_3(s):
        kind, fam, g = ORDER[s]
        arrive(db.at[s], rs_r.at[s, 2])
        arrive(da.at[s], rs_r.at[s, 3])
        arrive(ea.at[s], rs_r.at[s, 4])
        arrive(eb.at[s], rs_r.at[s, 5])
        pair = kind * 2 + g
        s2[pair, fam, 0:HC] = pown[s, 0:HC] + (ea[s].astype(F32) + da[s].astype(F32))
        s2[pair, fam, HC:CH] = pown[s, HC:CH] + (db[s].astype(F32) + eb[s].astype(F32))
        if fam == 1:
            mine = (yl + g + yh) % 2
            ysend[pair] = s2[pair, 1 - mine].astype(BF)
            send(ysend.at[pair], yrecv.at[pair], y_s.at[pair], y_r.at[pair], dev(yh=1 - yh))

    def finish(pair):
        kind, g = pair // 2, pair % 2
        mine = (yl + g + yh) % 2
        arrive(yrecv.at[pair], y_r.at[pair])
        total = s2[pair, mine] + yrecv[pair].astype(F32)
        zz = (z + ZOFF[kind]) % 4
        at = pl.ds(pl.multiple_of(zz * 64 + g * CH, CH), CH)
        u_ref[at, :] = (-total * mask[0:1, :]).astype(BF)

    def m_send(s, to, at, sem, lo=0, n=SUB):
        send(msub(s, lo, n), msub(at, lo, n), m_s.at[sem], m_r.at[sem], to)

    def on_arrival(b):
        if b == 0:
            arrive(msub(0), tx_r.at[0])
            m_send(0, dev(z=zp), 2, 2)
            m_send(0, dev(z=zm), 3, 3)
            m_send(0, dev(yl=1 - yl), 4, 4)
        elif b == 1:
            arrive(msub(1), tx_r.at[1])
            m_send(1, dev(z=zp), 5, 5)
            m_send(1, dev(z=zm), 6, 6)
            m_send(1, dev(yl=1 - yl), 7, 7)
        elif b in (2, 3):
            g = b - 2
            s0 = 2 + 3 * g
            for s in range(s0, s0 + 3):
                arrive(msub(s), m_r.at[s])
            m_send(s0, dev(z=zp), 8 + 4 * g, 8 + 4 * g, 0, 64)
            m_send(s0 + 1, dev(z=zm), 8 + 4 * g, 16 + g, 64, 64)
            m_send(s0 + 2, dev(z=zp), 9 + 4 * g, 9 + 4 * g)
            m_send(s0 + 2, dev(z=zm), 10 + 4 * g, 10 + 4 * g)
        elif b in (4, 6):
            g = (b - 4) // 2
            s = 8 + 4 * g
            arrive(msub(s, 0, 64), m_r.at[s])
            arrive(msub(s, 64, 64), m_r.at[16 + g])
            m_send(s, dev(yl=1 - yl), s + 3, s + 3)
        else:
            g = (b - 5) // 2
            for s in range(9 + 4 * g, 12 + 4 * g):
                arrive(msub(s), m_r.at[s])

    done = {}
    todo2, todo3 = [], []
    finished = []

    def run_3(s):
        reduce_3(s)
        kind, fam, g = ORDER[s]
        if fam == 1:
            finished.append(kind * 2 + g)

    for b, (s0, n) in enumerate(BATCHES):
        on_arrival(b)
        if b == 0:
            a_local.wait()
            arrive(afull.at[1 - h], a_sem.at[2])
        multiply(s0, n)
        for s in range(s0, s0 + n):
            reduce_1(s)
        for s in todo3:
            run_3(s)
        for s in todo2:
            reduce_2(s)
        todo3, todo2 = todo2, list(range(s0, s0 + n))
    for s in todo3:
        run_3(s)
    for s in todo2:
        reduce_2(s)
    for s in todo2:
        run_3(s)
    for pair in finished:
        finish(pair)

    corr = lax.dot_general(mt[...], u_ref[...], (((1,), (1,)), ((), ())), preferred_element_type=F32)
    dsend[...] = corr.astype(BF)

    def share(r):
        return pl.ds(pl.multiple_of(r * CH, CH), CH)

    def others():
        for k in range(1, 8):
            r = (row + k) % 8
            yield k, r, (r, col)

    for k, r, to in others():
        send(dsend.at[share(r)], drecv.at[8 - k], d_s.at[0, k], d_r.at[0, 8 - k], to)
    total = dsend[share(row), :].astype(F32)
    for k in range(1, 8):
        arrive(drecv.at[k], d_r.at[0, k])
        total += drecv[k].astype(F32)
    dfin[share(row), :] = total.astype(BF)
    for k, r, to in others():
        send(dfin.at[share(row)], dfin.at[share(row)], d_s.at[1, k], d_r.at[1, 8 - k], to)
    for k, r, to in others():
        arrive(dfin.at[share(r)], d_r.at[1, k])
    diag_ref[0] = dinv_ref[0] - dfin[...].astype(F32)

    for copy in sends:
        copy.wait_send()
    for here, far in tx_waits:
        @pl.when(jnp.logical_not(here))
        def _():
            far.wait_send()


def local(inverse_anc, factor_panel, pattern, diag_inverse):
    vmem = pl.BlockSpec(memory_space=pltpu.VMEM)
    dma = pltpu.SemaphoreType.DMA
    part = pltpu.VMEM((NSUB, HC, ROWS), BF)
    return pl.pallas_call(
        kernel,
        out_shape=(
            jax.ShapeDtypeStruct((SUPER, ROWS), BF),
            jax.ShapeDtypeStruct((1, SUPER, SUPER), F32),
        ),
        in_specs=[
            pl.BlockSpec(memory_space=pl.ANY),
            vmem,
            pl.BlockSpec(memory_space=pltpu.SMEM),
            vmem,
        ],
        out_specs=(vmem, vmem),
        scratch_shapes=[
            pltpu.VMEM((2, ROWS, HALF), BF),
            pltpu.VMEM((SUPER, ROWS), BF),
            pltpu.VMEM((8, ROWS), F32),
            pltpu.VMEM((2, 4, CH, ROWS), BF),
            pltpu.VMEM((NSUB * SUB, ROWS), BF),
            pltpu.VMEM((NSUB, 3 * CH, ROWS), BF),
            pltpu.VMEM((NSUB, CH, ROWS), F32),
            part, part, part, part, part, part,
            pltpu.VMEM((8, 2, CH, ROWS), F32),
            pltpu.VMEM((8, CH, ROWS), BF),
            pltpu.VMEM((8, CH, ROWS), BF),
            pltpu.VMEM((SUPER, SUPER), BF),
            pltpu.VMEM((8, CH, SUPER), BF),
            pltpu.VMEM((SUPER, SUPER), BF),
            dma((3,)),
            dma((2, 4)), dma((2, 4)),
            dma((2, 4)), dma((2,)),
            dma((18,)), dma((18,)),
            dma((NSUB, 6)), dma((NSUB, 6)),
            dma((8,)), dma((8,)),
            dma((2, 8)), dma((2, 8)),
        ],
        compiler_params=pltpu.CompilerParams(
            collective_id=0, has_side_effects=True, vmem_limit_bytes=60 << 20
        ),
        cost_estimate=pl.CostEstimate(flops=2 * 2048 * 2048 * 2048, bytes_accessed=8 << 20, transcendentals=0),
        name="selected_inverse",
    )(inverse_anc, factor_panel, pattern, diag_inverse)


def solution(mesh):
    return jax.shard_map(
        local,
        mesh=mesh,
        in_specs=(P("row", "col"), P("row", "col"), P(), P("col", None, None)),
        out_specs=(P("col", "row"), P("col", None, None)),
        check_vma=False,
    )
```

time: 652 us -> 140 us (0.21)
  waiting for transfers between devices: 489 us -> 0 us
  Pallas kernels: 0 us -> 133 us
  blocking collectives: 103 us -> 0 us
  matrix products: 26.3 us -> 0 us
  between operations: 13.8 us -> 0.64 us
  local copies, waits for them, and re-layouts: 12.4 us -> 3.97 us
  other arithmetic: 6.74 us -> 0 us
    reduce_scatter x1 -> x0, waiting for transfers between devices: 245 us -> none  [local(): lax.psum_scatter(lax.dot_general(spread, inverse_anc, (((0,), (1,)), ((),...]
    all_gather x1 -> x0, waiting for transfers between devices: 171 us -> none  [local(): panel = lax.all_gather(masked, 'row', axis=0, tiled=True)]
    pallas_call x0 -> x1, Pallas kernels: none -> 133 us  [local(): pl.pallas_call(kernel, out_shape=(jax.ShapeDtypeStruct((SUPER, ROWS), BF)...]
    all_to_all x1 -> x0, blocking collectives: 103 us -> none  [local(): lax.all_to_all(panel, 'col', split_axis=0, concat_axis=1, tiled=True)]
    psum x1 -> x0, waiting for transfers between devices: 73.5 us -> none  [local(): lax.psum(partial_diag.astype(jnp.bfloat16), 'row').astype(jnp.float32)]
    dot_general x2 -> x0, matrix products: 26.3 us -> none  [the longest x1 25.2 us: local(): lax.dot_general(spread, inverse_anc, (((0,), (1,)), ((), ())), preferred_...]
    all_to_all x1 -> x0, local copies, waits for them, and re-layouts: 12.3 us -> none  [local(): lax.all_to_all(panel, 'col', split_axis=0, concat_axis=1, tiled=True)]
  transfers between devices with their start and end apart: 3 -> 0, of which waited for: 3 -> 0; matrix products, arithmetic and copies ran while one was open for 0% -> 0% of each run, Pallas kernels for 0% -> 0%
where the time goes in v1:
time: 140 us; the launch traced here: 138 us
  Pallas kernels  133 us (95%)
  local copies, waits for them, and re-layouts  3.97 us (3%)
    pallas_call x1, Pallas kernels, local(): pl.pallas_call(kernel, out_shape=(jax.ShapeDtypeStruct((SUPER, ROWS), BF)...  133 us
    unnamed x2, local copies, waits for them, and re-layouts  3.97 us

profile of v1, /device:TPU:0, one launch (start us, length us, event | category | flops | bytes accessed | tf_op | source)
XLA Modules:
  0.0 137.5 jit_solution(3929899128126954083)
XLA Ops:
  0.6 132.9 %selected_inverse.1 = (bf16[256,2048]{1,0:T(8,128)(2,1)}, f32[1,256,256]{2,1,0:T(8,128)}) custom-call(bf16[2048,1024]{1,0:T(8,128)(2,1)} %a_ref.1, bf16[2048,256]{1,0:T(8,128)(2,1)} %f_ref.1, s32[16,64]{1,0:T(8,128)} %pat_ref.1, f32[1,256,256]{2,1,0:T(8,128)} %dinv_ref.1), custom_call_target="tpu_custom_call" | custom-call | flops 17179869184 | bytes 8388608 | tf_op jit(solution)/shard_map/selected_inverse/pallas_call | solution.py:286
  133.5 2.3 %copy.8 = bf16[256,2048]{1,0:T(8,128)(2,1)} copy(bf16[256,2048]{1,0:T(8,128)(2,1)} %get-tuple-element.4) | data formatting | bytes 2097152
  135.8 1.7 %copy.9 = f32[1,256,256]{2,1,0:T(8,128)} copy(f32[1,256,256]{2,1,0:T(8,128)} %get-tuple-element.5) | data formatting | bytes 524288

commit v2 on v0

v2 whole, which is shorter than its diff:
```python
import functools

import jax
import jax.numpy as jnp
from jax import lax
from jax.experimental import pallas as pl
from jax.experimental.pallas import tpu as pltpu
from jax.sharding import PartitionSpec as P

SUPER = 256
ROWS = 2048
HALF = 1024
GROUPS = 4
CH = 16
SUB = 4 * CH
NSUB = 8 * GROUPS
TILE = 256
BF = jnp.bfloat16
F32 = jnp.float32
MESH = pl.DeviceIdType.MESH

MEMBERS = {
    "own": ((0, 0),),
    "near": ((1, 0), (2, 0), (0, 1)),
    "two": ((3, 0),),
    "far": ((1, 1), (2, 1), (3, 1)),
}
LAYOUT = [
    ("own", 0), ("own", 1), ("own", 2), ("own", 3), ("near", 0), ("near", 1), ("near", 2), ("two", 0),
    ("far", 0), ("near", 3), ("two", 1), ("far", 1), ("two", 2), ("far", 2), ("two", 3), ("far", 3),
]
SHARDS = []
BASE = {}
for what, group in LAYOUT:
    BASE[what, group] = len(SHARDS)
    SHARDS += [(kind, fam, group) for kind, fam in MEMBERS[what]]
ZOFF = {0: 0, 1: 3, 2: 1, 3: 2}

UNITS = [(0, 1), (1, 1), (2, 1), (3, 1), (4, 3), (7, 3), (10, 4), (14, 3), (17, 4), (21, 4), (25, 4), (29, 1), (30, 1), (31, 1)]


def schedule():
    yield "over_x", 0
    yield "over_x", 1
    yield "over_x", 2
    yield "own", 0
    yield "over_x", 3
    yield "swap", 0
    yield "mul", (0, 1)
    yield "r1", 0
    for g in (1, 2, 3):
        yield "own", g
        yield "mul", (g, 1)
        yield "r1", g
        yield "r2", g - 1
    waits = {
        4: [("near", 0)], 5: [("near", 1)], 6: [("near", 2), ("two", 0)], 7: [("far", 0)],
        8: [("near", 3), ("two", 1)], 9: [("far", 1), ("two", 2)], 10: [("far", 2), ("two", 3)],
    }
    for u in range(4, 11):
        yield from waits[u]
        yield "mul", UNITS[u]
        yield "r1", u
        yield "r2", u - 1
        if u == 4:
            yield "r3", 0
            yield "r3", 1
        yield "r3", u - 2
        if u >= 8:
            yield "fin", u - 4
    yield "r2", 10
    yield "r3", 9
    yield "far", 3
    yield "mul", (29, 3)
    for u in (11, 12, 13):
        yield "r1", u
    yield "r3", 10
    for u in (11, 12, 13):
        yield "r2", u
    for u in (7, 8):
        yield "fin", u
    yield "fin", 9
    yield "r3", 11
    yield "fin", 10
    yield "r3", 12
    yield "r3", 13
    yield "send_early", 0
    for u in (11, 12, 13):
        yield "fin", u
    yield "sum_early", 0


def kernel(
    a_ref, f_hbm, pat_ref, dinv_hbm,
    u_hbm, diag_hbm,
    f_ref, dinv_ref, u_ref, diag_ref, afull, mt, mask, tz, m, p, pown, ra, rb, da, db, ea, eb, s2, ysend, yrecv, early, early_in, early_sum, late, corr,
    io_sem, u_sem, a_sem, tz_s, tz_r, tx_s, tx_r, m_s, m_r, rs_s, rs_r, y_s, y_r, d_s, d_r,
):
    row = lax.axis_index("row")
    col = lax.axis_index("col")
    z, yl = row // 2, row % 2
    x, yh, h = col // 4, (col // 2) % 2, col % 2

    def dev(z=z, yl=yl, x=x, yh=yh, h=h):
        return (z * 2 + yl, (x * 2 + yh) * 2 + h)

    def remote(src, dst, ssem, rsem, to):
        return pltpu.make_async_remote_copy(
            src_ref=src, dst_ref=dst, send_sem=ssem, recv_sem=rsem, device_id=to, device_id_type=MESH
        )

    def arrive(ref, sem):
        pltpu.make_async_copy(ref, ref, sem).wait()

    sends = []
    stores = []

    def send(src, dst, ssem, rsem, to):
        copy = remote(src, dst, ssem, rsem, to)
        copy.start()
        sends.append(copy)

    zp, zm = (z + 1) % 4, (z + 3) % 4
    xp, xm = (x + 1) % 4, (x + 3) % 4

    f_copy = pltpu.make_async_copy(f_hbm, f_ref, io_sem.at[0])
    f_copy.start()

    barrier = pltpu.get_barrier_semaphore()
    partners = [dev(h=1 - h), dev(yh=1 - yh)]
    for dz in range(4):
        for fl in range(2):
            if dz or fl:
                partners.append(dev(z=(z + dz) % 4, yl=(yl + fl) % 2))
    for dx in range(4):
        for fl in range(2):
            if dx or fl:
                partners.append(dev(x=(x + dx) % 4, yl=(yl + fl) % 2, yh=(yh + fl) % 2))
    for to in partners:
        pl.semaphore_signal(barrier, inc=1, device_id=to, device_id_type=MESH)

    a_local = pltpu.make_async_copy(a_ref, afull.at[h], a_sem.at[0])
    dinv_copy = pltpu.make_async_copy(dinv_hbm, dinv_ref, io_sem.at[1])
    f_copy.wait()
    a_local.start()
    dinv_copy.start()

    for b in range(8):
        keep = pat_ref[col, row * 8 + b].astype(F32)
        mask[:, b * 256:(b + 1) * 256] = jnp.full((8, 256), keep, F32)
        block = f_ref[b * 256:(b + 1) * 256, :].astype(F32)
        mt[:, b * 256:(b + 1) * 256] = (block.T * keep).astype(BF)

    pl.semaphore_wait(barrier, len(partners))

    def piece(zz, g):
        return mt.at[pl.ds(pl.multiple_of(zz * 64 + g * CH, CH), CH)]

    for g in range(GROUPS):
        for dz in (1, 3, 2) if g % 2 == 0 else (1, 3, 2, 0):
            zz = (z + dz) % 4
            k = (4 - dz) % 4
            to = dev(z=zz) if g % 2 == 0 else dev(z=zz, yl=1 - yl)
            send(piece(zz, g), tz.at[g, k], tz_s.at[g, k], tz_r.at[g, k], to)
    send(a_ref, afull.at[h], a_sem.at[1], a_sem.at[2], dev(h=1 - h))

    tx_waits = []
    def over_x(g):
        nyh, nyl = (yl, yh) if g % 2 == 0 else (1 - yl, 1 - yh)
        same_y = yl == yh if g % 2 == 0 else yl != yh
        for k in (0, 1, 3, 2):
            if g % 2 == 0 and k == 0:
                src = piece(z, g)
            else:
                src = tz.at[g, k]
                arrive(src, tz_r.at[g, k])
            xd = (z + k) % 4
            slot = (x + 4 - xd) % 4
            dst = m.at[pl.ds(pl.multiple_of(g * SUB + slot * CH, CH), CH)]
            remote_copy = remote(src, dst, tx_s.at[g, k], tx_r.at[g], dev(x=xd, yh=nyh, yl=nyl))
            local_copy = pltpu.make_async_copy(src, dst, tx_r.at[g])
            here = jnp.logical_and(same_y, xd == x)

            @pl.when(here)
            def _():
                local_copy.start()

            @pl.when(jnp.logical_not(here))
            def _():
                remote_copy.start()

            tx_waits.append((here, remote_copy))

    def msub(s, lo=0, n=SUB):
        return m.at[s * SUB + lo:s * SUB + lo + n]

    def multiply(s0, n):
        rows = slice(s0 * SUB, (s0 + n) * SUB)

        def tile(it, carry):
            at = pl.ds(pl.multiple_of(it * TILE, TILE), TILE)
            dims = (((1,), (1,)), ((), ()))
            acc = lax.dot_general(m[rows, :HALF], afull[0, at, :], dims, preferred_element_type=F32)
            acc += lax.dot_general(m[rows, HALF:], afull[1, at, :], dims, preferred_element_type=F32)
            for i in range(n):
                at_row = slice((s0 + i) * CH, (s0 + i + 1) * CH)
                pown[at_row, at] = acc[i * SUB:i * SUB + CH]
                for k in range(3):
                    lo = i * SUB + (k + 1) * CH
                    p[k, at_row, at] = acc[lo:lo + CH].astype(BF)
            return carry

        lax.fori_loop(0, ROWS // TILE, tile, 0)

    half = (slice(0, HALF), slice(HALF, ROWS))

    def rows_of(b):
        s0, n = UNITS[b]
        return slice(s0 * CH, (s0 + n) * CH)

    def x_send(b, i, src, dst, to):
        send(src, dst, rs_s.at[b, i], rs_r.at[b, i], to)

    def reduce_1(b):
        r = rows_of(b)
        x_send(b, 0, p.at[1, r, half[0]], ra.at[r], dev(x=xp))
        x_send(b, 1, p.at[1, r, half[1]], rb.at[r], dev(x=xm))
        x_send(b, 2, p.at[0, r, half[1]], db.at[r], dev(x=xp))
        x_send(b, 3, p.at[2, r, half[0]], da.at[r], dev(x=xm))

    def reduce_2(b):
        r = rows_of(b)
        arrive(ra.at[r], rs_r.at[b, 0])
        p[0, r, half[0]] = (p[0, r, half[0]].astype(F32) + ra[r].astype(F32)).astype(BF)
        x_send(b, 4, p.at[0, r, half[0]], ea.at[r], dev(x=xp))
        arrive(rb.at[r], rs_r.at[b, 1])
        p[2, r, half[1]] = (p[2, r, half[1]].astype(F32) + rb[r].astype(F32)).astype(BF)
        x_send(b, 5, p.at[2, r, half[1]], eb.at[r], dev(x=xm))

    def mine(g):
        return (yl + g + yh) % 2

    def reduce_3(b):
        r = rows_of(b)
        arrive(db.at[r], rs_r.at[b, 2])
        arrive(da.at[r], rs_r.at[b, 3])
        arrive(ea.at[r], rs_r.at[b, 4])
        arrive(eb.at[r], rs_r.at[b, 5])
        s0, n = UNITS[b]
        pairs = []
        for s in range(s0, s0 + n):
            kind, fam, g = SHARDS[s]
            pair = kind * GROUPS + g
            r = slice(s * CH, (s + 1) * CH)
            s2[pair, fam, :, half[0]] = pown[r, half[0]] + (ea[r].astype(F32) + da[r].astype(F32))
            s2[pair, fam, :, half[1]] = pown[r, half[1]] + (eb[r].astype(F32) + db[r].astype(F32))
            if fam == 1:
                ysend[pair] = s2[pair, 1 - mine(g)].astype(BF)
                send(ysend.at[pair], yrecv.at[pair], y_s.at[pair], y_r.at[pair], dev(yh=1 - yh))
                pairs.append(pair)
        return pairs

    def finish(pair):
        kind, g = pair // GROUPS, pair % GROUPS
        arrive(yrecv.at[pair], y_r.at[pair])
        total = s2[pair, mine(g)] + yrecv[pair].astype(F32)
        zz = (z + ZOFF[kind]) % 4
        at = pl.ds(pl.multiple_of(zz * 64 + g * CH, CH), CH)
        u_ref[at, :] = (-total * mask[0:1, :]).astype(BF)
        copy = pltpu.make_async_copy(u_ref.at[at], u_hbm.at[at], u_sem.at[pair])
        copy.start()
        stores.append(copy)

    def m_send(s, to, at, sem=None, lo=0, n=SUB):
        sem = at if sem is None else sem
        send(msub(s, lo, n), msub(at, lo, n), m_s.at[sem], m_r.at[sem], to)

    def arrival(what, g):
        s = BASE[what, g]
        if what == "own":
            to = BASE["near", g]
            arrive(msub(s), tx_r.at[g])
            m_send(s, dev(z=zp), to)
            m_send(s, dev(z=zm), to + 1)
            m_send(s, dev(yl=1 - yl), to + 2)
        elif what == "near":
            two, to = BASE["two", g], BASE["far", g]
            for i in range(3):
                arrive(msub(s + i), m_r.at[s + i])
            m_send(s, dev(z=zp), two, two, 0, SUB // 2)
            m_send(s + 1, dev(z=zm), two, NSUB + g, SUB // 2, SUB // 2)
            m_send(s + 2, dev(z=zp), to)
            m_send(s + 2, dev(z=zm), to + 1)
        elif what == "two":
            arrive(msub(s, 0, SUB // 2), m_r.at[s])
            arrive(msub(s, SUB // 2, SUB // 2), m_r.at[NSUB + g])
            m_send(s, dev(yl=1 - yl), BASE["far", g] + 2)
        else:
            for i in range(3):
                arrive(msub(s + i), m_r.at[s + i])

    def others():
        for k in range(1, 8):
            r = (row + k) % 8
            yield k, r, (r, col)

    def correction(lo, n):
        return lax.dot_general(u_ref[lo:lo + n], mt[...], (((1,), (1,)), ((), ())), preferred_element_type=F32)

    def share(r):
        return pl.ds(pl.multiple_of(r * 24, 8), 24)

    def send_early():
        for zz in range(4):
            early[zz * 48:(zz + 1) * 48] = correction(zz * 64, 48)
        for k, r, to in others():
            send(early.at[share(r)], early_in.at[8 - k], d_s.at[0, k], d_r.at[0, 8 - k], to)

    def sum_early():
        total = early[share(row), :]
        for k in range(1, 8):
            arrive(early_in.at[k], d_r.at[0, k])
            total += early_in[k]
        early_in[0] = total
        for k, r, to in others():
            send(early_in.at[0], early_sum.at[row], d_s.at[1, k], d_r.at[1, 8 - k], to)
        early_sum[row] = total

    def arrive_early():
        for k, r, to in others():
            arrive(early_sum.at[r], d_r.at[1, k])
        for zz in range(4):
            for i in range(2):
                lo = zz * 64 + i * 24
                corr[lo:lo + 24] = early_sum[zz * 2 + i]

    ready = {}
    for what, arg in schedule():
        if what == "over_x":
            over_x(arg)
        elif what == "swap":
            a_local.wait()
            arrive(afull.at[1 - h], a_sem.at[2])
        elif what == "mul":
            multiply(*arg)
        elif what == "r1":
            reduce_1(arg)
        elif what == "r2":
            reduce_2(arg)
        elif what == "r3":
            ready[arg] = reduce_3(arg)
        elif what == "send_early":
            send_early()
        elif what == "sum_early":
            sum_early()
        elif what == "fin":
            for pair in ready[arg]:
                finish(pair)
        else:
            arrival(what, arg)

    for zz in range(4):
        late[row, zz * CH:(zz + 1) * CH] = correction(zz * 64 + 48, CH).astype(BF)
    for k, r, to in others():
        send(late.at[row], late.at[row], d_s.at[2, k], d_r.at[2, 8 - k], to)
    arrive_early()
    for k, r, to in others():
        arrive(late.at[r], d_r.at[2, k])
    total = late[0].astype(F32)
    for r in range(1, 8):
        total += late[r].astype(F32)
    for zz in range(4):
        corr[zz * 64 + 48:(zz + 1) * 64] = total[zz * CH:(zz + 1) * CH]
    dinv_copy.wait()
    diag_ref[0] = dinv_ref[0] - corr[...].T
    copy = pltpu.make_async_copy(diag_ref, diag_hbm, io_sem.at[2])
    copy.start()
    stores.append(copy)

    for copy in stores:
        copy.wait()
    for copy in sends:
        copy.wait_send()
    for here, remote_copy in tx_waits:
        @pl.when(jnp.logical_not(here))
        def _():
            remote_copy.wait_send()


def place(u_in, diag_in, u_out, diag_out):
    u_out[...] = u_in[...]
    diag_out[...] = diag_in[...]


def local(inverse_anc, factor_panel, pattern, diag_inverse):
    hbm = pl.BlockSpec(memory_space=pl.ANY)
    dma = pltpu.SemaphoreType.DMA
    blocks = [pl.BlockSpec((64, ROWS), lambda i: (i, 0)), pl.BlockSpec((1, 64, SUPER), lambda i: (0, i, 0))]
    part = pltpu.VMEM((NSUB * CH, HALF), BF)
    out = pl.pallas_call(
        kernel,
        out_shape=(
            jax.ShapeDtypeStruct((SUPER, ROWS), BF),
            jax.ShapeDtypeStruct((1, SUPER, SUPER), F32),
        ),
        in_specs=[hbm, hbm, pl.BlockSpec(memory_space=pltpu.SMEM), hbm],
        out_specs=(hbm, hbm),
        scratch_shapes=[
            pltpu.VMEM((ROWS, SUPER), BF),
            pltpu.VMEM((1, SUPER, SUPER), F32),
            pltpu.VMEM((SUPER, ROWS), BF),
            pltpu.VMEM((1, SUPER, SUPER), F32),
            pltpu.VMEM((2, ROWS, HALF), BF),
            pltpu.VMEM((SUPER, ROWS), BF),
            pltpu.VMEM((8, ROWS), F32),
            pltpu.VMEM((GROUPS, 4, CH, ROWS), BF),
            pltpu.VMEM((NSUB * SUB, ROWS), BF),
            pltpu.VMEM((3, NSUB * CH, ROWS), BF),
            pltpu.VMEM((NSUB * CH, ROWS), F32),
            part, part, part, part, part, part,
            pltpu.VMEM((4 * GROUPS, 2, CH, ROWS), F32),
            pltpu.VMEM((4 * GROUPS, CH, ROWS), BF),
            pltpu.VMEM((4 * GROUPS, CH, ROWS), BF),
            pltpu.VMEM((192, SUPER), F32),
            pltpu.VMEM((8, 24, SUPER), F32),
            pltpu.VMEM((8, 24, SUPER), F32),
            pltpu.VMEM((8, 64, SUPER), BF),
            pltpu.VMEM((SUPER, SUPER), F32),
            dma((3,)), dma((4 * GROUPS,)),
            dma((3,)),
            dma((GROUPS, 4)), dma((GROUPS, 4)),
            dma((GROUPS, 4)), dma((GROUPS,)),
            dma((NSUB + GROUPS,)), dma((NSUB + GROUPS,)),
            dma((len(UNITS), 6)), dma((len(UNITS), 6)),
            dma((4 * GROUPS,)), dma((4 * GROUPS,)),
            dma((3, 8)), dma((3, 8)),
        ],
        compiler_params=pltpu.CompilerParams(
            collective_id=0, has_side_effects=True, vmem_limit_bytes=60 << 20
        ),
        cost_estimate=pl.CostEstimate(flops=2 * 2048 * 2048 * 2048, bytes_accessed=8 << 20, transcendentals=0),
        name="selected_inverse",
    )(inverse_anc, factor_panel, pattern, diag_inverse)
    return pl.pallas_call(
        place,
        out_shape=tuple(jax.ShapeDtypeStruct(o.shape, o.dtype) for o in out),
        grid=(4,),
        in_specs=blocks,
        out_specs=tuple(blocks),
        name="place_outputs",
    )(*out)


def solution(mesh):
    return jax.shard_map(
        local,
        mesh=mesh,
        in_specs=(P("row", "col"), P("row", "col"), P(), P("col", None, None)),
        out_specs=(P("col", "row"), P("col", None, None)),
        check_vma=False,
    )
```

time: 652 us -> 130 us (0.20)
  waiting for transfers between devices: 489 us -> 0 us
  Pallas kernels: 0 us -> 129 us
  blocking collectives: 103 us -> 0 us
  matrix products: 26.3 us -> 0 us
  between operations: 13.8 us -> 0.64 us
  local copies, waits for them, and re-layouts: 12.4 us -> 0 us
  other arithmetic: 6.74 us -> 0 us
    reduce_scatter x1 -> x0, waiting for transfers between devices: 245 us -> none  [local(): lax.psum_scatter(lax.dot_general(spread, inverse_anc, (((0,), (1,)), ((),...]
    all_gather x1 -> x0, waiting for transfers between devices: 171 us -> none  [local(): panel = lax.all_gather(masked, 'row', axis=0, tiled=True)]
    pallas_call x0 -> x2, Pallas kernels: none -> 129 us  [the longest x1 126 us: local(): pl.pallas_call(kernel, out_shape=(jax.ShapeDtypeStruct((SUPER, ROWS), BF)...]
    all_to_all x1 -> x0, blocking collectives: 103 us -> none  [local(): lax.all_to_all(panel, 'col', split_axis=0, concat_axis=1, tiled=True)]
    psum x1 -> x0, waiting for transfers between devices: 73.5 us -> none  [local(): lax.psum(partial_diag.astype(jnp.bfloat16), 'row').astype(jnp.float32)]
    dot_general x2 -> x0, matrix products: 26.3 us -> none  [the longest x1 25.2 us: local(): lax.dot_general(spread, inverse_anc, (((0,), (1,)), ((), ())), preferred_...]
    all_to_all x1 -> x0, local copies, waits for them, and re-layouts: 12.3 us -> none  [local(): lax.all_to_all(panel, 'col', split_axis=0, concat_axis=1, tiled=True)]
  transfers between devices with their start and end apart: 3 -> 0, of which waited for: 3 -> 0; matrix products, arithmetic and copies ran while one was open for 0% -> 0% of each run, Pallas kernels for 0% -> 0%
where the time goes in v2:
time: 130 us
  Pallas kernels  129 us (99%)
    pallas_call x1, Pallas kernels, local(): pl.pallas_call(kernel, out_shape=(jax.ShapeDtypeStruct((SUPER, ROWS), BF)...  126 us
    pallas_call x1, Pallas kernels, local(): pl.pallas_call(place, out_shape=tuple((jax.ShapeDtypeStruct(o.shape, o.dt...  3.41 us

profile of v2, /device:TPU:0, one launch (start us, length us, event | category | flops | bytes accessed | tf_op | source)
XLA Modules:
  0.0 130.0 jit_solution(14638351588877343524)
XLA Ops:
  0.6 125.9 %selected_inverse.1 = (bf16[256,2048]{1,0:T(8,128)(2,1)}, f32[1,256,256]{2,1,0:T(8,128)}) custom-call(bf16[2048,1024]{1,0:T(8,128)(2,1)} %a_ref.1, bf16[2048,256]{1,0:T(8,128)(2,1)} %f_hbm.1, s32[16,64]{1,0:T(8,128)} %pat_ref.1, f32[1,256,256]{2,1,0:T(8,128)} %dinv_hbm.1), custom_call_target="tpu_custom_call" | custom-call | flops 17179869184 | bytes 8388608 | tf_op jit(solution)/shard_map/selected_inverse/pallas_call | solution.py:400
  126.5 3.4 %place_outputs.1 = (bf16[256,2048]{1,0:T(8,128)(2,1)}, f32[1,256,256]{2,1,0:T(8,128)}) custom-call(bf16[256,2048]{1,0:T(8,128)(2,1)} %get-tuple-element.4.u_in, f32[1,256,256]{2,1,0:T(8,128)} %get-tuple-element.5.diag_in), custom_call_target="tpu_custom_call" | custom-call | tf_op jit(solution)/shard_map/place_outputs/pallas_call | solution.py:444

commit v3 on v2

--- a/solution.py
+++ b/solution.py
@@ -14,7 +14,7 @@
 CH = 16
 SUB = 4 * CH
 NSUB = 8 * GROUPS
-TILE = 256
+TILE = 1024
 BF = jnp.bfloat16
 F32 = jnp.float32
 MESH = pl.DeviceIdType.MESH
@@ -36,38 +36,75 @@
     SHARDS += [(kind, fam, group) for kind, fam in MEMBERS[what]]
 ZOFF = {0: 0, 1: 3, 2: 1, 3: 2}
 
+PATH = "abcb"
+FLIP = [int(path == "c") for path in PATH]
+
 UNITS = [(0, 1), (1, 1), (2, 1), (3, 1), (4, 3), (7, 3), (10, 4), (14, 3), (17, 4), (21, 4), (25, 4), (29, 1), (30, 1), (31, 1)]
 
 
 def schedule():
     yield "over_x", 0
+    yield "over_x", 2
     yield "over_x", 1
-    yield "over_x", 2
     yield "own", 0
     yield "over_x", 3
     yield "swap", 0
     yield "mul", (0, 1)
     yield "r1", 0
-    for g in (1, 2, 3):
-        yield "own", g
-        yield "mul", (g, 1)
-        yield "r1", g
-        yield "r2", g - 1
-    waits = {
-        4: [("near", 0)], 5: [("near", 1)], 6: [("near", 2), ("two", 0)], 7: [("far", 0)],
-        8: [("near", 3), ("two", 1)], 9: [("far", 1), ("two", 2)], 10: [("far", 2), ("two", 3)],
-    }
-    for u in range(4, 11):
-        yield from waits[u]
-        yield "mul", UNITS[u]
-        yield "r1", u
-        yield "r2", u - 1
-        if u == 4:
-            yield "r3", 0
-            yield "r3", 1
-        yield "r3", u - 2
-        if u >= 8:
-            yield "fin", u - 4
+    yield "own", 2
+    yield "own", 1
+    yield "mul", (1, 2)
+    yield "r1", 1
+    yield "r1", 2
+    yield "r2", 0
+    yield "own", 3
+    yield "r2", 1
+    yield "r2", 2
+    yield "r3", 0
+    yield "near", 0
+    yield "mul", (3, 4)
+    yield "r1", 3
+    yield "r1", 4
+    yield "r3", 1
+    yield "r2", 3
+    yield "near", 1
+    yield "mul", UNITS[5]
+    yield "r1", 5
+    yield "near", 2
+    yield "r2", 4
+    yield "r3", 2
+    yield "two", 0
+    yield "mul", UNITS[6]
+    yield "r1", 6
+    yield "r2", 5
+    yield "r3", 3
+    yield "near", 3
+    yield "far", 0
+    yield "mul", UNITS[7]
+    yield "r1", 7
+    yield "two", 1
+    yield "r2", 6
+    yield "r3", 4
+    yield "mul", UNITS[8]
+    yield "r1", 8
+    yield "two", 2
+    yield "r2", 7
+    yield "r3", 5
+    yield "fin", 4
+    yield "far", 1
+    yield "mul", UNITS[9]
+    yield "r1", 9
+    yield "two", 3
+    yield "r2", 8
+    yield "r3", 6
+    yield "fin", 5
+    yield "far", 2
+    yield "mul", UNITS[10]
+    yield "r1", 10
+    yield "r2", 9
+    yield "r3", 7
+    yield "fin", 6
+    yield "r3", 8
     yield "r2", 10
     yield "r3", 9
     yield "far", 3
@@ -77,17 +114,14 @@
     yield "r3", 10
     for u in (11, 12, 13):
         yield "r2", u
-    for u in (7, 8):
+    for u in (7, 8, 9, 10):
         yield "fin", u
-    yield "fin", 9
-    yield "r3", 11
-    yield "fin", 10
-    yield "r3", 12
-    yield "r3", 13
     yield "send_early", 0
     for u in (11, 12, 13):
+        yield "r3", u
+    yield "sum_early", 0
+    for u in (11, 12, 13):
         yield "fin", u
-    yield "sum_early", 0
 
 
 def kernel(
@@ -136,6 +170,8 @@
         for fl in range(2):
             if dx or fl:
                 partners.append(dev(x=(x + dx) % 4, yl=(yl + fl) % 2, yh=(yh + fl) % 2))
+    for dz in range(1, 4):
+        partners.append(dev(z=(z + dz) % 4, yl=1 - yl, yh=1 - yh))
     for to in partners:
         pl.semaphore_signal(barrier, inc=1, device_id=to, device_id_type=MESH)
 
@@ -156,20 +192,43 @@
     def piece(zz, g):
         return mt.at[pl.ds(pl.multiple_of(zz * 64 + g * CH, CH), CH)]
 
-    for g in range(GROUPS):
-        for dz in (1, 3, 2) if g % 2 == 0 else (1, 3, 2, 0):
+    tx_waits = []
+
+    def send_unless(here, src, dst, ssem, rsem, to):
+        remote_copy = remote(src, dst, ssem, rsem, to)
+        local_copy = pltpu.make_async_copy(src, dst, rsem)
+
+        @pl.when(here)
+        def _():
+            local_copy.start()
+
+        @pl.when(jnp.logical_not(here))
+        def _():
+            remote_copy.start()
+
+        tx_waits.append((here, remote_copy))
+
+    for g in (0, 2, 1, 3):
+        for dz in (1, 3, 2, 0):
             zz = (z + dz) % 4
             k = (4 - dz) % 4
-            to = dev(z=zz) if g % 2 == 0 else dev(z=zz, yl=1 - yl)
-            send(piece(zz, g), tz.at[g, k], tz_s.at[g, k], tz_r.at[g, k], to)
+            args = piece(zz, g), tz.at[g, k], tz_s.at[g, k], tz_r.at[g, k]
+            if PATH[g] == "a" and dz == 0:
+                send_unless(yl == yh, *args, dev(yh=yl, yl=yh))
+            elif PATH[g] == "a":
+                send(*args, dev(z=zz, yh=yl, yl=yh))
+            elif PATH[g] == "c":
+                send(*args, dev(z=zz, yl=1 - yl))
+            elif dz != 0:
+                send(*args, dev(z=zz))
     send(a_ref, afull.at[h], a_sem.at[1], a_sem.at[2], dev(h=1 - h))
 
-    tx_waits = []
     def over_x(g):
-        nyh, nyl = (yl, yh) if g % 2 == 0 else (1 - yl, 1 - yh)
-        same_y = yl == yh if g % 2 == 0 else yl != yh
+        path = PATH[g]
+        nyh, nyl = {"a": (yh, yl), "b": (yl, yh), "c": (1 - yl, 1 - yh)}[path]
+        same_y = {"a": True, "b": yl == yh, "c": yl != yh}[path]
         for k in (0, 1, 3, 2):
-            if g % 2 == 0 and k == 0:
+            if path == "b" and k == 0:
                 src = piece(z, g)
             else:
                 src = tz.at[g, k]
@@ -177,19 +236,8 @@
             xd = (z + k) % 4
             slot = (x + 4 - xd) % 4
             dst = m.at[pl.ds(pl.multiple_of(g * SUB + slot * CH, CH), CH)]
-            remote_copy = remote(src, dst, tx_s.at[g, k], tx_r.at[g], dev(x=xd, yh=nyh, yl=nyl))
-            local_copy = pltpu.make_async_copy(src, dst, tx_r.at[g])
             here = jnp.logical_and(same_y, xd == x)
-
-            @pl.when(here)
-            def _():
-                local_copy.start()
-
-            @pl.when(jnp.logical_not(here))
-            def _():
-                remote_copy.start()
-
-            tx_waits.append((here, remote_copy))
+            send_unless(here, src, dst, tx_s.at[g, k], tx_r.at[g], dev(x=xd, yh=nyh, yl=nyl))
 
     def msub(s, lo=0, n=SUB):
         return m.at[s * SUB + lo:s * SUB + lo + n]
@@ -197,20 +245,23 @@
     def multiply(s0, n):
         rows = slice(s0 * SUB, (s0 + n) * SUB)
 
-        def tile(it, carry):
-            at = pl.ds(pl.multiple_of(it * TILE, TILE), TILE)
-            dims = (((1,), (1,)), ((), ()))
-            acc = lax.dot_general(m[rows, :HALF], afull[0, at, :], dims, preferred_element_type=F32)
-            acc += lax.dot_general(m[rows, HALF:], afull[1, at, :], dims, preferred_element_type=F32)
-            for i in range(n):
-                at_row = slice((s0 + i) * CH, (s0 + i + 1) * CH)
-                pown[at_row, at] = acc[i * SUB:i * SUB + CH]
-                for k in range(3):
-                    lo = i * SUB + (k + 1) * CH
-                    p[k, at_row, at] = acc[lo:lo + CH].astype(BF)
-            return carry
-
-        lax.fori_loop(0, ROWS // TILE, tile, 0)
+        for hf in range(2):
+
+            def tile(it, carry):
+                col_at = pl.ds(pl.multiple_of(it * TILE, TILE), TILE)
+                at = pl.ds(pl.multiple_of(hf * HALF + it * TILE, TILE), TILE)
+                dims = (((1,), (1,)), ((), ()))
+                acc = lax.dot_general(m[rows, :HALF], afull[0, at, :], dims, preferred_element_type=F32)
+                acc += lax.dot_general(m[rows, HALF:], afull[1, at, :], dims, preferred_element_type=F32)
+                for i in range(n):
+                    at_row = slice((s0 + i) * CH, (s0 + i + 1) * CH)
+                    pown[at_row, at] = acc[i * SUB:i * SUB + CH]
+                    for k in range(3):
+                        lo = i * SUB + (k + 1) * CH
+                        p[k, hf, at_row, col_at] = acc[lo:lo + CH].astype(BF)
+                return carry
+
+            lax.fori_loop(0, HALF // TILE, tile, 0)
 
     half = (slice(0, HALF), slice(HALF, ROWS))
 
@@ -223,22 +274,22 @@
 
     def reduce_1(b):
         r = rows_of(b)
-        x_send(b, 0, p.at[1, r, half[0]], ra.at[r], dev(x=xp))
-        x_send(b, 1, p.at[1, r, half[1]], rb.at[r], dev(x=xm))
-        x_send(b, 2, p.at[0, r, half[1]], db.at[r], dev(x=xp))
-        x_send(b, 3, p.at[2, r, half[0]], da.at[r], dev(x=xm))
+        x_send(b, 0, p.at[1, 0, r], ra.at[r], dev(x=xp))
+        x_send(b, 1, p.at[1, 1, r], rb.at[r], dev(x=xm))
+        x_send(b, 2, p.at[0, 1, r], db.at[r], dev(x=xp))
+        x_send(b, 3, p.at[2, 0, r], da.at[r], dev(x=xm))
 
     def reduce_2(b):
         r = rows_of(b)
         arrive(ra.at[r], rs_r.at[b, 0])
-        p[0, r, half[0]] = (p[0, r, half[0]].astype(F32) + ra[r].astype(F32)).astype(BF)
-        x_send(b, 4, p.at[0, r, half[0]], ea.at[r], dev(x=xp))
+        p[0, 0, r] = (p[0, 0, r].astype(F32) + ra[r].astype(F32)).astype(BF)
+        x_send(b, 4, p.at[0, 0, r], ea.at[r], dev(x=xp))
         arrive(rb.at[r], rs_r.at[b, 1])
-        p[2, r, half[1]] = (p[2, r, half[1]].astype(F32) + rb[r].astype(F32)).astype(BF)
-        x_send(b, 5, p.at[2, r, half[1]], eb.at[r], dev(x=xm))
+        p[2, 1, r] = (p[2, 1, r].astype(F32) + rb[r].astype(F32)).astype(BF)
+        x_send(b, 5, p.at[2, 1, r], eb.at[r], dev(x=xm))
 
     def mine(g):
-        return (yl + g + yh) % 2
+        return (yl + FLIP[g] + yh) % 2
 
     def reduce_3(b):
         r = rows_of(b)
@@ -304,15 +355,15 @@
             r = (row + k) % 8
             yield k, r, (r, col)
 
-    def correction(lo, n):
-        return lax.dot_general(u_ref[lo:lo + n], mt[...], (((1,), (1,)), ((), ())), preferred_element_type=F32)
+    def correction(parts):
+        rows = jnp.concatenate([u_ref[lo:lo + n] for lo, n in parts], axis=0)
+        return lax.dot_general(rows, mt[...], (((1,), (1,)), ((), ())), preferred_element_type=F32)
 
     def share(r):
         return pl.ds(pl.multiple_of(r * 24, 8), 24)
 
     def send_early():
-        for zz in range(4):
-            early[zz * 48:(zz + 1) * 48] = correction(zz * 64, 48)
+        early[...] = correction([(zz * 64, 48) for zz in range(4)])
         for k, r, to in others():
             send(early.at[share(r)], early_in.at[8 - k], d_s.at[0, k], d_r.at[0, 8 - k], to)
 
@@ -359,8 +410,7 @@
         else:
             arrival(what, arg)
 
-    for zz in range(4):
-        late[row, zz * CH:(zz + 1) * CH] = correction(zz * 64 + 48, CH).astype(BF)
+    late[row] = correction([(zz * 64 + 48, CH) for zz in range(4)]).astype(BF)
     for k, r, to in others():
         send(late.at[row], late.at[row], d_s.at[2, k], d_r.at[2, 8 - k], to)
     arrive_early()
@@ -395,7 +445,7 @@
 def local(inverse_anc, factor_panel, pattern, diag_inverse):
     hbm = pl.BlockSpec(memory_space=pl.ANY)
     dma = pltpu.SemaphoreType.DMA
-    blocks = [pl.BlockSpec((64, ROWS), lambda i: (i, 0)), pl.BlockSpec((1, 64, SUPER), lambda i: (0, i, 0))]
+    blocks = [pl.BlockSpec((128, ROWS), lambda i: (i, 0)), pl.BlockSpec((1, 128, SUPER), lambda i: (0, i, 0))]
     part = pltpu.VMEM((NSUB * CH, HALF), BF)
     out = pl.pallas_call(
         kernel,
@@ -415,7 +465,7 @@
             pltpu.VMEM((8, ROWS), F32),
             pltpu.VMEM((GROUPS, 4, CH, ROWS), BF),
             pltpu.VMEM((NSUB * SUB, ROWS), BF),
-            pltpu.VMEM((3, NSUB * CH, ROWS), BF),
+            pltpu.VMEM((3, 2, NSUB * CH, HALF), BF),
             pltpu.VMEM((NSUB * CH, ROWS), F32),
             part, part, part, part, part, part,
             pltpu.VMEM((4 * GROUPS, 2, CH, ROWS), F32),
@@ -444,7 +494,7 @@
     return pl.pallas_call(
         place,
         out_shape=tuple(jax.ShapeDtypeStruct(o.shape, o.dtype) for o in out),
-        grid=(4,),
+        grid=(2,),
         in_specs=blocks,
         out_specs=tuple(blocks),
         name="place_outputs",

time: 130 us -> 126 us (0.969)
  Pallas kernels: 129 us -> 125 us
    pallas_call x1, Pallas kernels: 126 us -> 123 us  [local(): pl.pallas_call(kernel, out_shape=(jax.ShapeDtypeStruct((SUPER, ROWS), BF)...]
where the time goes in v3:
time: 126 us
  Pallas kernels  125 us (99%)
    pallas_call x1, Pallas kernels, local(): pl.pallas_call(kernel, out_shape=(jax.ShapeDtypeStruct((SUPER, ROWS), BF)...  123 us

profile of v3, /device:TPU:0, one launch (start us, length us, event | category | flops | bytes accessed | tf_op | source)
XLA Modules:
  0.0 125.5 jit_solution(9790991263201630791)
XLA Ops:
  0.6 122.7 %selected_inverse.1 = (bf16[256,2048]{1,0:T(8,128)(2,1)}, f32[1,256,256]{2,1,0:T(8,128)}) custom-call(bf16[2048,1024]{1,0:T(8,128)(2,1)} %a_ref.1, bf16[2048,256]{1,0:T(8,128)(2,1)} %f_hbm.1, s32[16,64]{1,0:T(8,128)} %pat_ref.1, f32[1,256,256]{2,1,0:T(8,128)} %dinv_hbm.1), custom_call_target="tpu_custom_call" | custom-call | flops 17179869184 | bytes 8388608 | tf_op jit(solution)/shard_map/selected_inverse/pallas_call | solution.py:450
  123.4 2.2 %place_outputs.1 = (bf16[256,2048]{1,0:T(8,128)(2,1)}, f32[1,256,256]{2,1,0:T(8,128)}) custom-call(bf16[256,2048]{1,0:T(8,128)(2,1)} %get-tuple-element.4.u_in, f32[1,256,256]{2,1,0:T(8,128)} %get-tuple-element.5.diag_in), custom_call_target="tpu_custom_call" | custom-call | tf_op jit(solution)/shard_map/place_outputs/pallas_call | solution.py:494

commit v4 on v3

--- a/solution.py
+++ b/solution.py
@@ -80,6 +80,7 @@
     yield "r3", 3
     yield "near", 3
     yield "far", 0
+    yield "mark", 0
     yield "mul", UNITS[7]
     yield "r1", 7
     yield "two", 1
@@ -105,6 +106,8 @@
     yield "r3", 7
     yield "fin", 6
     yield "r3", 8
+    yield "drain", 0
+    yield "mark", 0
     yield "r2", 10
     yield "r3", 9
     yield "far", 3
@@ -116,6 +119,7 @@
         yield "r2", u
     for u in (7, 8, 9, 10):
         yield "fin", u
+    yield "drain", 0
     yield "send_early", 0
     for u in (11, 12, 13):
         yield "r3", u
@@ -207,6 +211,11 @@
             remote_copy.start()
 
         tx_waits.append((here, remote_copy))
+
+    def wait_unless(here, remote_copy):
+        @pl.when(jnp.logical_not(here))
+        def _():
+            remote_copy.wait_send()
 
     for g in (0, 2, 1, 3):
         for dz in (1, 3, 2, 0):
@@ -386,6 +395,7 @@
                 corr[lo:lo + 24] = early_sum[zz * 2 + i]
 
     ready = {}
+    drained = marked = 0
     for what, arg in schedule():
         if what == "over_x":
             over_x(arg)
@@ -400,6 +410,15 @@
             reduce_2(arg)
         elif what == "r3":
             ready[arg] = reduce_3(arg)
+        elif what == "mark":
+            marked = len(sends)
+        elif what == "drain":
+            for copy in sends[drained:marked]:
+                copy.wait_send()
+            drained = marked
+            for here, remote_copy in tx_waits:
+                wait_unless(here, remote_copy)
+            tx_waits.clear()
         elif what == "send_early":
             send_early()
         elif what == "sum_early":
@@ -429,12 +448,8 @@
 
     for copy in stores:
         copy.wait()
-    for copy in sends:
+    for copy in sends[drained:]:
         copy.wait_send()
-    for here, remote_copy in tx_waits:
-        @pl.when(jnp.logical_not(here))
-        def _():
-            remote_copy.wait_send()
 
 
 def place(u_in, diag_in, u_out, diag_out):

time: 126 us -> 126 us (level)
  no operation moved by 1% of the time
where the time goes in v4:
time: 126 us; the launch traced here: 125 us
  Pallas kernels  125 us (99%)
    pallas_call x1, Pallas kernels, local(): pl.pallas_call(kernel, out_shape=(jax.ShapeDtypeStruct((SUPER, ROWS), BF)...  123 us

profile of v4, /device:TPU:0, one launch (start us, length us, event | category | flops | bytes accessed | tf_op | source)
XLA Modules:
  0.0 125.4 jit_solution(13969041641611137681)
XLA Ops:
  0.6 122.6 %selected_inverse.1 = (bf16[256,2048]{1,0:T(8,128)(2,1)}, f32[1,256,256]{2,1,0:T(8,128)}) custom-call(bf16[2048,1024]{1,0:T(8,128)(2,1)} %a_ref.1, bf16[2048,256]{1,0:T(8,128)(2,1)} %f_hbm.1, s32[16,64]{1,0:T(8,128)} %pat_ref.1, f32[1,256,256]{2,1,0:T(8,128)} %dinv_hbm.1), custom_call_target="tpu_custom_call" | custom-call | flops 17179869184 | bytes 8388608 | tf_op jit(solution)/shard_map/selected_inverse/pallas_call | solution.py:465
  123.2 2.2 %place_outputs.1 = (bf16[256,2048]{1,0:T(8,128)(2,1)}, f32[1,256,256]{2,1,0:T(8,128)}) custom-call(bf16[256,2048]{1,0:T(8,128)(2,1)} %get-tuple-element.4.u_in, f32[1,256,256]{2,1,0:T(8,128)} %get-tuple-element.5.diag_in), custom_call_target="tpu_custom_call" | custom-call | tf_op jit(solution)/shard_map/place_outputs/pallas_call | solution.py:509
